TPU v7x, 32 devices: a whole 2x2x4 slice. The times are simulated.
32 devices in a mesh: dp: 2 (over core), ctx: 8 (over z, y), exp: 2 (over x).
Axes of the slice: x: 2, y: 2, z: 4, core: 2. Of those that a mesh axis runs over, the one named last changes fastest.
Arguments:
- tokens: bfloat16 [2, 1024, 2560], P('dp', 'ctx'), may hold values from -6 to 6
- queries: bfloat16 [2, 1024, 16, 576], P('dp', 'ctx', 'exp'), may hold values from -240 to 240
- kv_weight: bfloat16 [2560, 576], P('exp'), may hold values from -0.125 to 0.125
- kv_gain: bfloat16 [512], replicated, may hold values from 0.5 to 1.5
- uv_weight: bfloat16 [16, 512, 128], P('exp'), may hold values from -0.75 to 0.75
- out_weight: bfloat16 [2048, 2560], P('exp'), may hold values from -0.5 to 0.5
- post_gain: bfloat16 [2560], replicated, may hold values from 0.5 to 1.5
- router_weight: bfloat16 [2560, 16], replicated, may hold values from -0.125 to 0.125
- expert_ids: int32 [2, 1024, 6], P('dp', 'ctx'), may hold values from 0 to 15, all different within a row; in each aligned block of 128 rows (0 to 127, 128 to 255, ..., all dimensions but the last counted through in order) at most 64 rows name the same one
- doc_ids: int32 [2, 1024], P('dp', 'ctx'), may hold values from 0 to 3, never falling along the last dimension, each value on 1 to 512 neighbouring positions
- gate_weight: bfloat16 [16, 2560, 1536], P('ctx', None, 'exp'), may hold values from -0.125 to 0.125
- up_weight: bfloat16 [16, 2560, 1536], P('ctx', None, 'exp'), may hold values from -0.125 to 0.125
- down_weight: bfloat16 [16, 1536, 2560], P('ctx', 'exp'), may hold values from -0.15625 to 0.15625
- cotangent: bfloat16 [2, 1024, 2560], P('dp', 'ctx'), may hold values from -6 to 6
Outputs:
- layer_out: bfloat16 [2, 1024, 2560], P('dp', 'ctx')
- router_grad: float32 [2560, 16], replicated
- gate_grad: bfloat16 [16, 2560, 1536], P('ctx', 'dp', 'exp')
- up_grad: bfloat16 [16, 2560, 1536], P('ctx', 'dp', 'exp')
- down_grad: bfloat16 [16, 1536, 2560], P('ctx', 'exp', 'dp')
Inputs may be any that keep to these rules, and one draw needn't show every extreme that they name: `expert_ids`: in each aligned block of 128 positions of a sequence no expert is named by more than 64 of the block's assignments; the experts of one token differ. `doc_ids`: document numbers never fall along a sequence; a document has at most 512 positions.
All inputs are finite; a program needn't handle non-finite values.
Results may differ from a plain program's by a relative error of at most 0.023.
The roundings to bfloat16 on the way count: a program that leaves them out, or rounds other values in their place, can miss the bound.
Values may be sent and summed in bfloat16 or wider, within the bound.
A program may use at most 192 MiB of HBM per device.

v0:
```python
import jax
import jax.numpy as jnp
from jax import lax
from jax.sharding import PartitionSpec as P

ROPE = 64
NOPE = 128


epsilon = 1e-06


def rms_scale(values, gain):
    return values * lax.rsqrt(jnp.mean(values * values, axis=-1, keepdims=True) + epsilon) * gain


def rotate(rope_part, positions):
    half_width = rope_part.shape[-1] // 2
    frequency = jnp.power(
        10000.0, -2.0 * jnp.arange(half_width, dtype=jnp.float32) / rope_part.shape[-1]
    )
    angles = positions.astype(jnp.float32)[:, None] * frequency[None, :]
    cosine = jnp.cos(angles)
    sine_part = jnp.sin(angles)
    first_half = rope_part[:, :half_width]
    second = rope_part[:, half_width:]
    return jnp.concatenate(
        [first_half * cosine - second * sine_part, second * cosine + first_half * sine_part], axis=1
    )


def route_slots(outgoing):
    moved = lax.all_to_all(outgoing, "ctx", split_axis=0, concat_axis=0, tiled=True)
    return moved


def local(
    tokens,
    queries,
    kv_weight,
    kv_gain,
    uv_weight,
    out_weight,
    post_gain,
    router_weight,
    expert_ids,
    doc_ids,
    gate_weight,
    up_weight,
    down_weight,
    cotangent,
):
    local_rows = tokens[0]
    seq_rows = local_rows.shape[0]
    model_width = local_rows.shape[1]
    latent_width = kv_gain.shape[0]
    row_share = kv_weight.shape[0]
    columns = lax.dynamic_slice_in_dim(local_rows, lax.axis_index("exp") * row_share, row_share, 1)
    compressed = lax.psum(jnp.dot(columns, kv_weight, preferred_element_type=jnp.float32), "exp")
    positions = lax.axis_index("ctx") * seq_rows + jnp.arange(seq_rows, dtype=jnp.int32)
    latent = rms_scale(compressed[:, :latent_width], kv_gain.astype(jnp.float32)).astype(
        jnp.bfloat16
    )
    rope_key = rotate(compressed[:, latent_width:], positions).astype(jnp.bfloat16)
    key_rows = jnp.concatenate([latent, rope_key], axis=1)
    all_keys, all_docs = (
        lax.all_gather(key_rows, "ctx", axis=0, tiled=True),
        lax.all_gather(doc_ids[0], "ctx", axis=0, tiled=True),
    )
    key_positions = jnp.arange(all_keys.shape[0], dtype=jnp.int32)
    allowed = (key_positions[None, :] <= positions[:, None]) & (
        all_docs[None, :] == doc_ids[0][:, None]
    )
    allowed = allowed[:, None, :]
    score_scale = (NOPE + ROPE) ** (-0.5)
    scores = (
        jnp.einsum("qhd,kd->qhk", queries[0], all_keys, preferred_element_type=jnp.float32)
        * score_scale
    )
    score_peak = jnp.max(jnp.where(allowed, scores, -1e30), axis=-1, keepdims=True)
    weights = jnp.exp(jnp.where(allowed, scores - score_peak, -1e30))
    weight_total = jnp.sum(weights, axis=-1, keepdims=True)
    mixed_latent = (
        jnp.einsum(
            "qhk,kl->qhl",
            weights.astype(jnp.bfloat16),
            all_keys[:, :latent_width],
            preferred_element_type=jnp.float32,
        )
        / weight_total
    )
    mixed_latent = mixed_latent.astype(jnp.bfloat16)
    head_values = (
        jnp.einsum("qhl,hlv->qhv", mixed_latent, uv_weight, preferred_element_type=jnp.float32)
        .astype(jnp.bfloat16)
        .reshape(seq_rows, -1)
    )
    head_part = jnp.dot(head_values, out_weight, preferred_element_type=jnp.float32)
    attention = lax.psum(head_part, "exp")
    hidden = (local_rows.astype(jnp.float32) + attention).astype(jnp.bfloat16)
    normed = rms_scale(hidden.astype(jnp.float32), post_gain.astype(jnp.float32)).astype(
        jnp.bfloat16
    )
    logits = jnp.dot(normed, router_weight, preferred_element_type=jnp.float32)
    router_probs = jax.nn.softmax(logits, axis=-1)
    picked_ids = expert_ids[0]
    experts_all = router_weight.shape[1]
    top_count = picked_ids.shape[1]
    chosen = jnp.take_along_axis(router_probs, picked_ids, axis=1)
    chosen_sum = jnp.sum(chosen, axis=1, keepdims=True)
    route_w = chosen / chosen_sum
    route_wb = route_w.astype(jnp.bfloat16)
    ctx_count = lax.axis_size("ctx")
    held_experts = experts_all // ctx_count
    capacity = (4 * seq_rows * top_count + 3 * experts_all - 1) // (3 * experts_all)
    flat_ids = picked_ids.reshape(-1)
    onehot = (flat_ids[:, None] == jnp.arange(experts_all, dtype=jnp.int32)[None, :]).astype(
        jnp.int32
    )
    slot_rank = jnp.sum((jnp.cumsum(onehot, axis=0) - onehot) * onehot, axis=1).reshape(
        seq_rows, top_count
    )
    slot_index = picked_ids * capacity + slot_rank
    slot_hits = (
        slot_index[:, :, None] == jnp.arange(experts_all * capacity, dtype=jnp.int32)[None, None, :]
    )
    dispatch = jnp.any(slot_hits, axis=1).astype(jnp.bfloat16)
    combine = jnp.sum(
        jnp.where(slot_hits, route_wb[:, :, None], jnp.zeros((), jnp.bfloat16)), axis=1
    )
    outgoing = jnp.einsum("se,sd->ed", dispatch, normed, preferred_element_type=jnp.float32).astype(
        jnp.bfloat16
    )
    outgoing = outgoing.reshape(-1, held_experts, capacity, model_width)
    arrived = route_slots(outgoing)
    gate_pre = jnp.einsum(
        "sjcd,jdf->sjcf", arrived, gate_weight, preferred_element_type=jnp.float32
    )
    up_pre = jnp.einsum("sjcd,jdf->sjcf", arrived, up_weight, preferred_element_type=jnp.float32)
    activated = (jax.nn.silu(gate_pre) * up_pre).astype(jnp.bfloat16)
    expert_part = jnp.einsum(
        "sjcf,jfd->sjcd", activated, down_weight, preferred_element_type=jnp.float32
    ).astype(jnp.bfloat16)
    returned = lax.all_to_all(expert_part, "ctx", split_axis=0, concat_axis=0, tiled=True)
    returned = returned.reshape(experts_all * capacity, model_width)
    moe_part = jnp.dot(combine, returned, preferred_element_type=jnp.float32)
    cot_rows = cotangent[0]
    cross_terms = jnp.einsum("sd,ed->se", cot_rows, returned, preferred_element_type=jnp.float32)
    dweight_part = jnp.take_along_axis(cross_terms, slot_index, axis=1)
    moe, dweight = lax.psum((moe_part, dweight_part), "exp")
    layer_out = (hidden.astype(jnp.float32) + moe).astype(jnp.bfloat16)
    mean_term = jnp.sum(dweight * route_w, axis=1, keepdims=True)
    dchosen = (dweight - mean_term) / chosen_sum
    id_hits = (
        picked_ids[:, :, None] == jnp.arange(experts_all, dtype=jnp.int32)[None, None, :]
    ).astype(jnp.float32)
    dprobs = jnp.sum(id_hits * dchosen[:, :, None], axis=1)
    dlogits = router_probs * (dprobs - jnp.sum(router_probs * dprobs, axis=1, keepdims=True))
    router_term = jnp.dot(normed.astype(jnp.float32).T, dlogits, precision=lax.Precision.HIGHEST)
    router_grad = lax.psum(router_term, ("dp", "ctx"))
    slot_cot = jnp.einsum(
        "se,sd->ed", combine, cot_rows, preferred_element_type=jnp.float32
    ).astype(jnp.bfloat16)
    slot_cot = slot_cot.reshape(-1, held_experts, capacity, model_width)
    cot_arrived = route_slots(slot_cot)
    down_term = jnp.einsum(
        "sjcf,sjcd->jfd", activated, cot_arrived, preferred_element_type=jnp.float32
    )
    dact = jnp.einsum(
        "sjcd,jfd->sjcf", cot_arrived, down_weight, preferred_element_type=jnp.float32
    )
    sigmoid_gate = jax.nn.sigmoid(gate_pre)
    dgate = (dact * up_pre * sigmoid_gate * (1.0 + gate_pre * (1.0 - sigmoid_gate))).astype(
        jnp.bfloat16
    )
    dup = (dact * gate_pre * sigmoid_gate).astype(jnp.bfloat16)
    gate_term = jnp.einsum("sjcd,sjcf->jdf", arrived, dgate, preferred_element_type=jnp.float32)
    up_term = jnp.einsum("sjcd,sjcf->jdf", arrived, dup, preferred_element_type=jnp.float32)
    gate_sum, up_sum, down_sum = (
        lax.psum_scatter(gate_term, "dp", scatter_dimension=1, tiled=True),
        lax.psum_scatter(up_term, "dp", scatter_dimension=1, tiled=True),
        lax.psum_scatter(down_term, "dp", scatter_dimension=2, tiled=True),
    )
    gate_out = gate_sum.astype(jnp.bfloat16)
    up_out = up_sum.astype(jnp.bfloat16)
    down_out = down_sum.astype(jnp.bfloat16)
    return (layer_out[None], router_grad, gate_out, up_out, down_out)


def solution(mesh):
    placed = (
        P("dp", "ctx", None),
        P("dp", "ctx", "exp", None),
        P("exp", None),
        P(),
        P("exp", None, None),
        P("exp", None),
        P(),
        P(),
        P("dp", "ctx", None),
        P("dp", "ctx"),
        P("ctx", None, "exp"),
        P("ctx", None, "exp"),
        P("ctx", "exp", None),
        P("dp", "ctx", None),
    )
    return jax.shard_map(
        local,
        mesh=mesh,
        in_specs=placed,
        out_specs=(
            P("dp", "ctx", None),
            P(),
            P("ctx", "dp", "exp"),
            P("ctx", "dp", "exp"),
            P("ctx", "exp", "dp"),
        ),
        check_vma=False,
    )
```

profile of v0, /device:TPU:8, one launch (start us, length us, event | category | flops | bytes accessed | tf_op | source)
XLA Modules:
  0.0 765.1 jit_solution(12009317812304315604)
XLA Ops:
  7.3 1.3 copy-done
  8.5 2.2 fusion.64
  10.9 0.7 convert_element_type.99
  11.6 24.2 %all-reduce.5.cloned.1.call-done = f32[128,576]{0,1:T(8,128)} async-done(((f32[128,576]{0,1:T(8,128)}), f32[128,576]{0,1:T(8,128)}) %all-reduce.5.cloned.1.call-update) | async-done | bytes 294928 | tf_op jit(solution)/shard_map/psum | solution.py:59
  35.8 1.0 multiply_reduce_fusion
  36.8 0.9 fusion.83
  37.7 1.1 multiply_convert_fusion
  38.8 0.7 pad_maximum_fusion
  39.5 17.7 %all-gather = s32[1,1024]{1,0:T(1,128)S(1)} all-gather(s32[1,128]{1,0:T(1,128)S(1)} %copy-done.7), channel_id=2, replica_groups=mesh['dp'=2,'ctx'=8,'exp'=2] {'ctx'}, dimensions={1}, use_global_device_ids=true | all-gather | bytes 4608 | tf_op jit(solution)/shard_map/all_gather | solution.py:68
  57.2 0.2 fusion.63
  57.4 22.5 %all-gather.3.cloned.1.call-done = bf16[1024,576]{0,1:T(8,128)(2,1)} async-done(((bf16[128,576]{0,1:T(8,128)(2,1)}), bf16[1024,576]{0,1:T(8,128)(2,1)}) %all-gather.3.cloned.1.call-update) | async-done | bytes 1179664 | tf_op jit(solution)/shard_map/all_gather | solution.py:67
  79.9 3.1 fusion.56
  83.0 3.4 fusion.103
  86.4 3.4 fusion.53
  89.9 4.5 fusion.105
  94.4 0.1 copy.72
  94.5 0.1 eq.75
  94.6 0.1 eq.71
  94.8 1.7 reduce-window.6
  96.5 0.3 slice_reduce_fusion
  96.8 0.1 fusion.76
  96.9 0.1 reshape.242
  97.1 0.5 fusion.33
  97.6 42.2 %all-reduce.7.cloned.1.call-done = f32[128,2560]{1,0:T(8,128)} async-done(((f32[128,2560]{1,0:T(8,128)}), f32[128,2560]{1,0:T(8,128)}) %all-reduce.7.cloned.1.call-update) | async-done | bytes 1310736 | tf_op jit(solution)/shard_map/psum | solution.py:99
  139.9 1.6 fusion.43
  141.5 3.9 convolution_convert_fusion.1
  145.4 6.4 all-to-all-start
  151.8 0.1 reshape.245
  152.0 0.1 reshape.248
  152.2 0.4 fusion.104
  152.6 5.1 gather_fusion
  157.7 0.1 reshape.251
  158.0 0.4 fusion.40
  158.4 3.9 convolution_convert_fusion
  162.3 102.6 %all-to-all-done = bf16[8,2,64,2560]{3,2,1,0:T(8,128)(2,1)} async-done(((bf16[8,2,64,2560]{3,2,1,0:T(8,128)(2,1)}), bf16[8,2,64,2560]{3,2,1,0:T(8,128)(2,1)}, u32[]{:S(2)}, u32[]{:S(2)}) %all-to-all-start) | async-done | bytes 5242912 | tf_op jit(solution)/shard_map/all_to_all | solution.py:33
  265.0 7.1 all-to-all-start.2
  272.1 10.7 %fusion.1 = f32[2,8,64,768]{3,2,1,0:T(8,128)} fusion(bf16[2,2560,768]{2,1,0:T(8,128)(2,1)} %param.25, bf16[8,2,64,2560]{3,2,1,0:T(8,128)(2,1)} %all-to-all-done), kind=kOutput, calls=%fused_computation.6 | convolution fusion | flops 4026531840 | bytes 16252928 | tf_op jit(solution)/shard_map/sjcd,jdf->sjcf/dot_general | solution.py:139
  282.7 10.7 %fusion.3 = f32[2,8,64,768]{3,2,1,0:T(8,128)} fusion(bf16[2,2560,768]{2,1,0:T(8,128)(2,1)} %param.24, bf16[8,2,64,2560]{3,2,1,0:T(8,128)(2,1)} %all-to-all-done), kind=kOutput, calls=%fused_computation.8 | convolution fusion | flops 4026531840 | bytes 16252928 | tf_op jit(solution)/shard_map/sjcd,jdf->sjcf/dot_general | solution.py:136
  293.4 91.1 %all-to-all-done.2 = bf16[8,2,64,2560]{3,2,1,0:T(8,128)(2,1)} async-done(((bf16[8,2,64,2560]{3,2,1,0:T(8,128)(2,1)}), bf16[8,2,64,2560]{3,2,1,0:T(8,128)(2,1)}, u32[]{:S(2)}, u32[]{:S(2)}) %all-to-all-start.2) | async-done | bytes 5242912 | tf_op jit(solution)/shard_map/all_to_all | solution.py:33
  384.5 14.0 %fusion.27 = (bf16[8,2,64,768]{3,2,0,1:T(8,128)(2,1)}, bf16[8,2,64,768]{3,2,0,1:T(8,128)(2,1)}, bf16[8,2,64,768]{3,2,0,1:T(8,128)(2,1)}) fusion(f32[2,8,64,768]{3,2,1,0:T(8,128)} %fusion.3, f32[2,8,64,768]{3,2,1,0:T(8,128)} %fusion.1, bf16[2,768,2560]{2,1,0:T(8,128)(2,1)} %param.26, bf16[8,2,64,2560]{3,2,1,0:T(8,128)(2,1)} %all-to-all-done.2), kind=kOutput, calls=%fused_computation.34 | convolution fusion | flops 4039114752 | bytes 24117248 | tf_op jit(solution)/shard_map/sjcd,jfd->sjcf/dot_general | solution.py:169
  398.5 8.0 %fusion.12 = bf16[8,2,64,2560]{3,2,0,1:T(8,128)(2,1)S(1)} fusion(bf16[8,2,64,768]{3,2,0,1:T(8,128)(2,1)} %get-tuple-element.9, bf16[2,768,2560]{2,1,0:T(8,128)(2,1)} %param.26), kind=kOutput, calls=%fused_computation.17 | convolution fusion | flops 4029153280 | bytes 14680064 | tf_op jit(solution)/shard_map/sjcf,jfd->sjcd/dot_general | solution.py:141
  406.5 0.5 copy.80
  406.9 121.1 %all_to_all.15 = bf16[8,2,64,2560]{3,2,1,0:T(8,128)(2,1)S(1)} all-to-all(bf16[8,2,64,2560]{3,2,1,0:T(8,128)(2,1)S(1)} %copy.80), channel_id=1, replica_groups=mesh['dp'=2,'ctx'=8,'exp'=2] {'ctx'}, dimensions={0} | all-to-all | bytes 10485760 | tf_op jit(solution)/shard_map/all_to_all | solution.py:144
  528.0 2.3 copy-done.2
  530.3 1.9 fusion.106
  532.3 12.8 %convolution_bitcast_fusion.2 = f32[2,768,2560]{2,1,0:T(8,128)} fusion(bf16[8,2,64,768]{3,2,0,1:T(8,128)(2,1)} %get-tuple-element.9, bf16[8,2,64,2560]{3,2,1,0:T(8,128)(2,1)} %all-to-all-done.2), kind=kOutput, calls=%fused_computation.5 | convolution fusion | flops 4026531840 | bytes 22544384 | tf_op jit(solution)/shard_map/sjcf,sjcd->jfd/dot_general | solution.py:166
  545.2 12.8 %convolution_bitcast_fusion = f32[2,2560,768]{2,1,0:T(8,128)} fusion(bf16[8,2,64,2560]{3,2,1,0:T(8,128)(2,1)} %all-to-all-done, bf16[8,2,64,768]{3,2,0,1:T(8,128)(2,1)} %get-tuple-element.7), kind=kOutput, calls=%fused_computation.3 | convolution fusion | flops 4026531840 | bytes 22544384 | tf_op jit(solution)/shard_map/sjcd,sjcf->jdf/dot_general | solution.py:178
  558.0 0.3 reduce-scatter.4.cloned.1.call-start
  558.3 13.1 %convolution_bitcast_fusion.1 = f32[2,2560,768]{2,1,0:T(8,128)} fusion(bf16[8,2,64,2560]{3,2,1,0:T(8,128)(2,1)} %all-to-all-done, bf16[8,2,64,768]{3,2,0,1:T(8,128)(2,1)} %get-tuple-element.8), kind=kOutput, calls=%fused_computation.4 | convolution fusion | flops 4026531840 | bytes 22544384 | tf_op jit(solution)/shard_map/sjcd,sjcf->jdf/dot_general | solution.py:177
  571.4 0.1 reshape.254
  571.6 4.0 convolution_bitcast_fusion.3
  575.6 5.1 gather_fusion.1
  580.7 0.1 reshape.257
  580.9 4.9 psum.38
  585.9 1.2 fusion.86
  587.2 2.6 fusion.60
  589.8 14.6 %reduce-scatter.8.cloned.1.call-done = f32[2,768,1280]{2,1,0:T(8,128)} async-done(((f32[2,768,2560]{2,1,0:T(8,128)}), f32[2,768,1280]{2,1,0:T(8,128)}) %reduce-scatter.8.cloned.1.call-update) | async-done | bytes 7864336 | tf_op jit(solution)/shard_map/reduce_scatter | solution.py:182
  604.3 5.5 convert_element_type.123
  609.9 23.0 %reduce-scatter.6.cloned.1.call-done = f32[2,1280,768]{2,1,0:T(8,128)} async-done(((f32[2,2560,768]{2,1,0:T(8,128)}), f32[2,1280,768]{2,1,0:T(8,128)}) %reduce-scatter.6.cloned.1.call-update) | async-done | bytes 7864336 | tf_op jit(solution)/shard_map/reduce_scatter | solution.py:181
  632.9 5.6 convert_element_type.122
  638.6 23.0 %reduce-scatter.4.cloned.1.call-done = f32[2,1280,768]{2,1,0:T(8,128)} async-done(((f32[2,2560,768]{2,1,0:T(8,128)}), f32[2,1280,768]{2,1,0:T(8,128)}) %reduce-scatter.4.cloned.1.call-update) | async-done | bytes 7864336 | tf_op jit(solution)/shard_map/reduce_scatter | solution.py:180
  661.6 5.5 convert_element_type.120
  667.1 89.1 %all-reduce.11.cloned.1.call-done = f32[2560,16]{0,1:T(8,128)} async-done(((f32[2560,16]{0,1:T(8,128)}), f32[2560,16]{0,1:T(8,128)}) %all-reduce.11.cloned.1.call-update) | async-done | bytes 163856 | tf_op jit(solution)/shard_map/psum | solution.py:160
  756.2 1.6 copy.127
  (61 shorter events, 0.9 us)
Async XLA Ops:
  7.2 1.4 copy-start
  7.2 32.3 %copy-start.7 = (s32[1,128]{1,0:T(1,128)S(1)}, s32[1,128]{1,0:T(1,128)}, u32[]{:S(2)}) copy-start(s32[1,128]{1,0:T(1,128)} %param.23) | copy-start | bytes 1540
  7.2 72.7 %copy-start.8 = (bf16[1,128,8,576]{1,3,2,0:T(8,128)(2,1)S(1)}, bf16[1,128,8,576]{1,3,2,0:T(8,128)(2,1)}, u32[]{:S(2)}) copy-start(bf16[1,128,8,576]{1,3,2,0:T(8,128)(2,1)} %param.15) | copy-start | bytes 3538948
  7.2 28.6 %all-reduce.5.cloned.1.call-start = ((), (), s32[]{:S(2)}) async-start(), calls=%async_computation.6 | async-start | bytes 589824 | tf_op jit(solution)/shard_map/psum | solution.py:59
  10.8 69.1 %all-gather.3.cloned.1.call-start = ((), (), s32[]{:S(2)}) async-start(), calls=%async_computation.7 | async-start | bytes 1327104 | tf_op jit(solution)/shard_map/all_gather | solution.py:67
  39.5 100.4 %all-reduce.7.cloned.1.call-start = ((), (), s32[]{:S(2)}) async-start(), calls=%async_computation.8 | async-start | bytes 2621440 | tf_op jit(solution)/shard_map/psum | solution.py:99
  83.0 3.4 copy-start.9
  83.0 3.4 copy-start.10
  89.8 4.5 copy-start.5
  89.9 4.9 copy-start.6
  89.9 50.0 %copy-start.4 = (bf16[1,128,2560]{2,1,0:T(8,128)(2,1)S(1)}, bf16[1,128,2560]{2,1,0:T(8,128)(2,1)}, u32[]{:S(2)}) copy-start(bf16[1,128,2560]{2,1,0:T(8,128)(2,1)} %param.14) | copy-start | bytes 1966084
  145.4 6.8 copy-start.11
  145.4 119.5 %all-to-all-start = ((bf16[8,2,64,2560]{3,2,1,0:T(8,128)(2,1)}), bf16[8,2,64,2560]{3,2,1,0:T(8,128)(2,1)}, u32[]{:S(2)}, u32[]{:S(2)}) async-start(bf16[8,2,64,2560]{3,2,1,0:T(8,128)(2,1)} %bitcast.182), calls=%async_computation | async-start | bytes 10485760 | tf_op jit(solution)/shard_map/all_to_all | solution.py:33
  152.6 5.8 copy-start.3
  265.0 119.6 %all-to-all-start.2 = ((bf16[8,2,64,2560]{3,2,1,0:T(8,128)(2,1)}), bf16[8,2,64,2560]{3,2,1,0:T(8,128)(2,1)}, u32[]{:S(2)}, u32[]{:S(2)}) async-start(bf16[8,2,64,2560]{3,2,1,0:T(8,128)(2,1)} %bitcast.183), calls=%async_computation.2 | async-start | bytes 10485760 | tf_op jit(solution)/shard_map/all_to_all | solution.py:33
  272.0 315.1 %all-reduce.9.cloned.1.call-start = ((), (), s32[]{:S(2)}) async-start(), calls=%async_computation.9 | async-start | bytes 2621440 | tf_op jit(solution)/shard_map/psum | solution.py:150
  528.0 2.3 copy-start.2
  532.3 72.1 %reduce-scatter.8.cloned.1.call-start = ((), (), s32[]{:S(2)}) async-start(), calls=%async_computation.13 | async-start | bytes 23592960 | tf_op jit(solution)/shard_map/reduce_scatter | solution.py:182
  545.1 87.8 %reduce-scatter.6.cloned.1.call-start = ((), (), s32[]{:S(2)}) async-start(), calls=%async_computation.12 | async-start | bytes 23592960 | tf_op jit(solution)/shard_map/reduce_scatter | solution.py:181
  558.0 103.6 %reduce-scatter.4.cloned.1.call-start = ((), (), s32[]{:S(2)}) async-start(), calls=%async_computation.11 | async-start | bytes 23592960 | tf_op jit(solution)/shard_map/reduce_scatter | solution.py:180
  571.4 184.8 %all-reduce.11.cloned.1.call-start = ((), (), s32[]{:S(2)}) async-start(), calls=%async_computation.10 | async-start | bytes 327680 | tf_op jit(solution)/shard_map/psum | solution.py:160
  632.9 124.9 %copy-start.1 = (bf16[1280,576]{0,1:T(8,128)(2,1)S(1)}, bf16[1280,576]{0,1:T(8,128)(2,1)}, u32[]{:S(2)}) copy-start(bf16[1280,576]{0,1:T(8,128)(2,1)} %param.16) | copy-start | bytes 4423684
Sparse Core Ops, SparseCore 0:
  10.9 24.7 all-reduce.4
  39.6 40.2 all-gather.2
  94.5 45.3 all-reduce.6
  532.4 44.2 all-reduce.8
  578.8 25.4 reduce-scatter.7
  606.5 26.3 reduce-scatter.5
  635.2 26.3 reduce-scatter.3
  665.6 90.5 all-reduce.10
where the time goes:
time: 773 us; the launch traced here: 765 us
  waiting for transfers between devices  433 us (56%)
  blocking collectives  144 us (19%)
  matrix products  110 us (14%)
  other arithmetic  31.9 us (4%)
  local copies, waits for them, and re-layouts  17.5 us (2%)
  between operations  14.9 us (2%)
  starting transfers between devices  14 us (2%)
    all_to_all x2, waiting for transfers between devices, route_slots(): lax.all_to_all(outgoing, 'ctx', split_axis=0, concat_axis=0, tiled=True)  194 us
    all_to_all x1, blocking collectives, local(): lax.all_to_all(expert_part, 'ctx', split_axis=0, concat_axis=0, tiled=True)  121 us
    psum x1, waiting for transfers between devices, local(): router_grad = lax.psum(router_term, ('dp', 'ctx'))  89.1 us
    psum x1, waiting for transfers between devices, local(): attention = lax.psum(head_part, 'exp')  42.2 us
    psum x1, waiting for transfers between devices, local(): lax.psum(jnp.dot(columns, kv_weight, preferred_element_type=jnp.float32),...  24.2 us
    reduce_scatter x1, waiting for transfers between devices, local(): lax.psum_scatter(gate_term, 'dp', scatter_dimension=1, tiled=True)  23 us
    reduce_scatter x1, waiting for transfers between devices, local(): lax.psum_scatter(up_term, 'dp', scatter_dimension=1, tiled=True)  23 us
    all_gather x1, waiting for transfers between devices, local(): lax.all_gather(key_rows, 'ctx', axis=0, tiled=True)  22.5 us
  transfers between devices with their start and end apart: 10, of which 9 were waited for; matrix products, arithmetic and copies ran while one was open for 14% of the time, Pallas kernels for 0%

commit v1 on v0

v1 whole, which is shorter than its diff:
```python
import jax
import jax.numpy as jnp
from jax import lax
from jax.sharding import PartitionSpec as P

ROPE = 64
NOPE = 128


epsilon = 1e-06


def rms_scale(values, gain):
    return values * lax.rsqrt(jnp.mean(values * values, axis=-1, keepdims=True) + epsilon) * gain


def rotate(rope_part, positions):
    half_width = rope_part.shape[-1] // 2
    frequency = jnp.power(
        10000.0, -2.0 * jnp.arange(half_width, dtype=jnp.float32) / rope_part.shape[-1]
    )
    angles = positions.astype(jnp.float32)[:, None] * frequency[None, :]
    cosine = jnp.cos(angles)
    sine_part = jnp.sin(angles)
    first_half = rope_part[:, :half_width]
    second = rope_part[:, half_width:]
    return jnp.concatenate(
        [first_half * cosine - second * sine_part, second * cosine + first_half * sine_part], axis=1
    )


def from_peer(values, axis):
    return lax.ppermute(values, axis, [(0, 1), (1, 0)])


def sum_over(values, axis):
    if lax.axis_size(axis) == 2:
        return values + from_peer(values, axis)
    return lax.psum(values, axis)


def scatter_rows(values, axis):
    if lax.axis_size(axis) > 2:
        return lax.psum_scatter(values, axis, scatter_dimension=0, tiled=True)
    share = values.shape[0] // 2
    at = lax.axis_index(axis)
    own = lax.dynamic_slice_in_dim(values, at * share, share, 0)
    sent = lax.dynamic_slice_in_dim(values, (1 - at) * share, share, 0)
    return own + from_peer(sent, axis)


def split_parts(values):
    high = lax.reduce_precision(values, 8, 7)
    rest = values - high
    middle = lax.reduce_precision(rest, 8, 7)
    return jnp.concatenate([high, middle, rest - middle], axis=1).astype(jnp.bfloat16)


def local(
    tokens,
    queries,
    kv_weight,
    kv_gain,
    uv_weight,
    out_weight,
    post_gain,
    router_weight,
    expert_ids,
    doc_ids,
    gate_weight,
    up_weight,
    down_weight,
    cotangent,
):
    bf16, f32 = jnp.bfloat16, jnp.float32
    local_rows = tokens[0]
    seq_rows = local_rows.shape[0]
    half_rows = seq_rows // lax.axis_size("exp")
    model_width = local_rows.shape[1]
    half_width = model_width // 2
    latent_width = kv_gain.shape[0]
    row_share = kv_weight.shape[0]
    dp_at, ctx_at, exp_at = (lax.axis_index(name) for name in ("dp", "ctx", "exp"))
    ctx_count = lax.axis_size("ctx")

    cot_all = lax.all_gather(cotangent[0], "ctx", axis=0, tiled=True)

    columns = lax.dynamic_slice_in_dim(local_rows, exp_at * row_share, row_share, 1)
    compressed = jnp.dot(columns, kv_weight, preferred_element_type=f32)
    compressed = sum_over(compressed, "exp")
    positions = ctx_at * seq_rows + jnp.arange(seq_rows, dtype=jnp.int32)
    latent = rms_scale(compressed[:, :latent_width], kv_gain.astype(f32)).astype(bf16)
    rope_key = rotate(compressed[:, latent_width:], positions).astype(bf16)
    key_width = latent_width + rope_key.shape[1]
    key_rows = jnp.concatenate(
        [latent, rope_key, expert_ids[0].astype(bf16), doc_ids[0][:, None].astype(bf16)], axis=1
    )
    gathered = lax.all_gather(key_rows, "ctx", axis=0, tiled=True)
    all_keys = gathered[:, :key_width]
    ids_all = gathered[:, key_width:-1].astype(jnp.int32)
    all_docs = gathered[:, -1].astype(jnp.int32)

    experts_all = router_weight.shape[1]
    top_count = ids_all.shape[1]
    held = experts_all // ctx_count
    capacity = (4 * seq_rows * top_count + 3 * experts_all - 1) // (3 * experts_all)
    member = jnp.any(
        ids_all[:, :, None] == jnp.arange(experts_all, dtype=jnp.int32)[None, None, :], axis=1
    )
    member_f = member.astype(f32)
    member_own = lax.dynamic_slice_in_dim(member_f, ctx_at * held, held, 1).reshape(
        ctx_count, seq_rows, held
    )
    before = jnp.tril(jnp.ones((seq_rows, seq_rows), bf16), -1)
    rank = jnp.einsum(
        "ut,stj->sju", before, member_own.astype(bf16), preferred_element_type=f32
    ).astype(jnp.int32)
    hits = (rank[:, :, None, :] == jnp.arange(capacity, dtype=jnp.int32)[None, None, :, None]) & (
        jnp.moveaxis(member_own, 1, 2)[:, :, None, :] > 0
    )
    dispatch = hits.astype(bf16).reshape(ctx_count, held * capacity, seq_rows)

    def to_slots(rows):
        return jnp.einsum(
            "sct,std->scd",
            dispatch,
            rows.reshape(ctx_count, seq_rows, model_width),
            preferred_element_type=f32,
        ).astype(bf16).reshape(ctx_count, held, capacity, model_width)

    def own_half(rows):
        return lax.dynamic_slice_in_dim(rows, dp_at * half_width, half_width, rows.ndim - 1)

    def peer_half(rows):
        other = lax.dynamic_slice_in_dim(rows, (1 - dp_at) * half_width, half_width, rows.ndim - 1)
        return from_peer(other, "dp")

    allowed = (jnp.arange(all_keys.shape[0], dtype=jnp.int32)[None, :] <= positions[:, None]) & (
        all_docs[None, :] == doc_ids[0][:, None]
    )
    allowed = allowed[:, None, :]
    score_scale = (NOPE + ROPE) ** (-0.5)
    scores = (
        jnp.einsum("qhd,kd->qhk", queries[0], all_keys, preferred_element_type=f32) * score_scale
    )
    score_peak = jnp.max(jnp.where(allowed, scores, -1e30), axis=-1, keepdims=True)
    weights = jnp.exp(jnp.where(allowed, scores - score_peak, -1e30))
    weight_total = jnp.sum(weights, axis=-1, keepdims=True)
    mixed_latent = (
        jnp.einsum(
            "qhk,kl->qhl",
            weights.astype(bf16),
            all_keys[:, :latent_width],
            preferred_element_type=f32,
        )
        / weight_total
    ).astype(bf16)
    head_values = (
        jnp.einsum("qhl,hlv->qhv", mixed_latent, uv_weight, preferred_element_type=f32)
        .astype(bf16)
        .reshape(seq_rows, -1)
    )
    head_part = jnp.dot(head_values, out_weight, preferred_element_type=f32)
    attention = scatter_rows(head_part, "exp")
    token_rows = lax.dynamic_slice_in_dim(local_rows, exp_at * half_rows, half_rows, 0)
    hidden = (token_rows.astype(f32) + attention).astype(bf16)
    normed = rms_scale(hidden.astype(f32), post_gain.astype(f32)).astype(bf16)
    normed_all = lax.all_gather(normed, ("ctx", "exp"), axis=0, tiled=True)

    cot_slots = to_slots(cot_all)
    cot_peer = peer_half(cot_slots)
    dact_raw = jnp.einsum("sjcd,jfd->sjcf", cot_slots, down_weight, preferred_element_type=f32)

    arrived = to_slots(normed_all)
    arrived_peer = peer_half(arrived)
    logits = jnp.dot(normed_all, router_weight, preferred_element_type=f32)
    router_probs = jax.nn.softmax(logits, axis=-1)
    chosen = router_probs * member_f
    chosen_sum = jnp.sum(chosen, axis=1, keepdims=True)
    route_w = chosen / chosen_sum
    route_own = lax.dynamic_slice_in_dim(route_w, ctx_at * held, held, 1).reshape(
        ctx_count, seq_rows, held
    )
    route_own = lax.reduce_precision(jnp.moveaxis(route_own, 1, 2), 8, 7)
    slot_w = jnp.sum(jnp.where(hits, route_own[:, :, None, :], 0.0), axis=3)
    combine = jnp.where(hits, route_own[:, :, None, :], 0.0).astype(bf16).reshape(
        ctx_count, held * capacity, seq_rows
    )

    gate_pre = jnp.einsum("sjcd,jdf->sjcf", arrived, gate_weight, preferred_element_type=f32)
    up_pre = jnp.einsum("sjcd,jdf->sjcf", arrived, up_weight, preferred_element_type=f32)
    sigmoid_gate = jax.nn.sigmoid(gate_pre)
    activated = (gate_pre * sigmoid_gate * up_pre).astype(bf16)
    expert_part = jnp.einsum(
        "sjcf,jfd->sjcd", activated, down_weight, preferred_element_type=f32
    ).astype(bf16)
    moe_part = jnp.einsum(
        "sct,scd->std",
        combine,
        expert_part.reshape(ctx_count, held * capacity, model_width),
        preferred_element_type=f32,
    ).astype(bf16)
    moe = lax.psum_scatter(
        moe_part.reshape(-1, model_width), ("ctx", "exp"), scatter_dimension=0, tiled=True
    )

    weighted = (activated.astype(f32) * slot_w[..., None]).astype(bf16)
    dact = dact_raw * slot_w[..., None]
    dgate = (dact * up_pre * sigmoid_gate * (1.0 + gate_pre * (1.0 - sigmoid_gate))).astype(bf16)
    dup = (dact * gate_pre * sigmoid_gate).astype(bf16)
    weighted_peer, dgate_peer, dup_peer = (
        from_peer(weighted, "dp"),
        from_peer(dgate, "dp"),
        from_peer(dup, "dp"),
    )

    dweight_slot = jnp.sum(activated.astype(f32) * dact_raw, axis=-1)
    dweight_part = jnp.sum(jnp.where(hits, dweight_slot[..., None], 0.0), axis=2)
    dweight_part = jnp.moveaxis(dweight_part, 1, 2).reshape(-1, held)
    dweight_each = lax.all_gather(dweight_part.T, ("ctx", "exp"), axis=0, tiled=False)
    dweight_each = dweight_each.reshape(ctx_count, -1, held, dweight_part.shape[0])
    dweight = jnp.sum(dweight_each, axis=1).reshape(experts_all, -1).T
    mean_term = jnp.sum(dweight * route_w, axis=1, keepdims=True)
    dprobs = member_f * (dweight - mean_term) / chosen_sum
    dlogits = router_probs * (dprobs - jnp.sum(router_probs * dprobs, axis=1, keepdims=True))
    router_parts = jnp.einsum(
        "td,te->de", normed_all, split_parts(dlogits), preferred_element_type=f32
    )
    router_term = jnp.sum(router_parts.reshape(model_width, 3, experts_all), axis=1)
    router_grad = router_term + from_peer(router_term, "dp")

    def summed(form, own, own_other, peer, peer_other):
        first = jnp.einsum(form, own, own_other, preferred_element_type=f32)
        second = jnp.einsum(form, peer, peer_other, preferred_element_type=f32)
        return (first + second).astype(bf16)

    arrived_own = own_half(arrived)
    gate_out = summed("sjcd,sjcf->jdf", arrived_own, dgate, arrived_peer, dgate_peer)
    up_out = summed("sjcd,sjcf->jdf", arrived_own, dup, arrived_peer, dup_peer)
    down_out = summed("sjcf,sjcd->jfd", weighted, own_half(cot_slots), weighted_peer, cot_peer)

    layer_half = (hidden.astype(f32) + moe.astype(f32)).astype(bf16)
    layer_out = lax.all_gather(layer_half, "exp", axis=0, tiled=True)
    return (layer_out[None], router_grad, gate_out, up_out, down_out)


def solution(mesh):
    placed = (
        P("dp", "ctx", None),
        P("dp", "ctx", "exp", None),
        P("exp", None),
        P(),
        P("exp", None, None),
        P("exp", None),
        P(),
        P(),
        P("dp", "ctx", None),
        P("dp", "ctx"),
        P("ctx", None, "exp"),
        P("ctx", None, "exp"),
        P("ctx", "exp", None),
        P("dp", "ctx", None),
    )
    return jax.shard_map(
        local,
        mesh=mesh,
        in_specs=placed,
        out_specs=(
            P("dp", "ctx", None),
            P(),
            P("ctx", "dp", "exp"),
            P("ctx", "dp", "exp"),
            P("ctx", "exp", "dp"),
        ),
        check_vma=False,
    )
```

time: 773 us -> 426 us (0.55)
  waiting for transfers between devices: 433 us -> 212 us
  blocking collectives: 144 us -> 54.1 us
  other arithmetic: 31.9 us -> 17.8 us
  starting transfers between devices: 14 us -> 4.72 us
    all_to_all x2 -> x0, waiting for transfers between devices: 194 us -> none  [route_slots(): lax.all_to_all(outgoing, 'ctx', split_axis=0, concat_axis=0, tiled=True)]
    psum x4 -> x0, waiting for transfers between devices: 156 us -> none  [the longest x1 89.1 us: local(): router_grad = lax.psum(router_term, ('dp', 'ctx'))]
    all_gather x1 -> x3, waiting for transfers between devices: 22.5 us -> 176 us  [the longest x1 81.3 us: local(): normed_all = lax.all_gather(normed, ('ctx', 'exp'), axis=0, tiled=True)]
    all_to_all x1 -> x0, blocking collectives: 121 us -> none  [local(): lax.all_to_all(expert_part, 'ctx', split_axis=0, concat_axis=0, tiled=True)]
    reduce_scatter x3 -> x1, waiting for transfers between devices: 60.6 us -> 15.6 us  [local(): lax.psum_scatter(moe_part.reshape(-1, model_width), ('ctx', 'exp'), scatt...]
    all_gather x1 -> x2, blocking collectives: 17.7 us -> 54.1 us  [the longest x1 42.6 us: local(): lax.all_gather(dweight_part.T, ('ctx', 'exp'), axis=0, tiled=False)]
    ppermute x0 -> x8, waiting for transfers between devices: none -> 20.1 us  [from_peer(): return lax.ppermute(values, axis, [(0, 1), (1, 0)])]
    all_to_all x2 -> x0, starting transfers between devices: 13.5 us -> none  [route_slots(): lax.all_to_all(outgoing, 'ctx', split_axis=0, concat_axis=0, tiled=True)]
  transfers between devices with their start and end apart: 10 -> 12, of which waited for: 9 -> 6; matrix products, arithmetic and copies ran while one was open for 14% -> 19% of each run, Pallas kernels for 0% -> 0%
where the time goes in v1:
time: 426 us; the launch traced here: 419 us
  waiting for transfers between devices  212 us (50%)
  matrix products  105 us (25%)
  blocking collectives  54.1 us (13%)
  other arithmetic  17.8 us (4%)
  between operations  14.5 us (3%)
  local copies, waits for them, and re-layouts  10.8 us (3%)
  starting transfers between devices  4.72 us (1%)
    all_gather x1, waiting for transfers between devices, local(): normed_all = lax.all_gather(normed, ('ctx', 'exp'), axis=0, tiled=True)  81.3 us
    all_gather x1, waiting for transfers between devices, local(): cot_all = lax.all_gather(cotangent[0], 'ctx', axis=0, tiled=True)  53.5 us
    all_gather x1, blocking collectives, local(): lax.all_gather(dweight_part.T, ('ctx', 'exp'), axis=0, tiled=False)  42.6 us
    all_gather x1, waiting for transfers between devices, local(): gathered = lax.all_gather(key_rows, 'ctx', axis=0, tiled=True)  40.9 us
    dot_general x3, matrix products, summed(): second = jnp.einsum(form, peer, peer_other, preferred_element_type=f32)  22.3 us
    ppermute x8, waiting for transfers between devices, from_peer(): return lax.ppermute(values, axis, [(0, 1), (1, 0)])  20.1 us
    dot_general x3, matrix products, summed(): first = jnp.einsum(form, own, own_other, preferred_element_type=f32)  17 us
    reduce_scatter x1, waiting for transfers between devices, local(): lax.psum_scatter(moe_part.reshape(-1, model_width), ('ctx', 'exp'), scatt...  15.6 us
  transfers between devices with their start and end apart: 12, of which 6 were waited for; matrix products, arithmetic and copies ran while one was open for 19% of the time, Pallas kernels for 0%

profile of v1, /device:TPU:8, one launch (start us, length us, event | category | flops | bytes accessed | tf_op | source)
XLA Modules:
  0.0 419.2 jit_solution(9602530112547193458)
XLA Ops:
  7.3 1.3 copy-done
  8.5 1.5 fusion.66
  10.1 1.6 collective-permute-start
  11.6 0.7 convert_element_type.144
  12.3 0.7 convert_bitcast_fusion
  13.0 0.7 fusion.104
  13.7 5.2 %collective-permute-done = f32[128,576]{0,1:T(8,128)S(1)} collective-permute-done((f32[128,576]{0,1:T(8,128)S(1)}, f32[128,576]{0,1:T(8,128)S(1)}, u32[]{:S(2)}, u32[]{:S(2)}) %collective-permute-start) | collective-permute-done | bytes 294944 | tf_op jit(solution)/shard_map/ppermute | solution.py:33
  18.9 0.1 multiply_reduce_fusion
  19.0 0.1 multiply_convert_fusion
  19.1 0.1 fusion.93
  19.3 2.5 concatenate.10
  21.9 0.7 all-gather.11.cloned.1.call-update
  22.6 40.9 %all-gather.7.cloned.1.call-done = bf16[1024,583]{0,1:T(8,128)(2,1)} async-done(((bf16[128,583]{0,1:T(8,128)(2,1)}), bf16[1024,583]{0,1:T(8,128)(2,1)}) %all-gather.7.cloned.1.call-update) | async-done | bytes 1194000 | tf_op jit(solution)/shard_map/all_gather | solution.py:98
  63.5 0.7 slice_convert_fusion.1
  64.2 0.2 fusion.62
  64.4 3.1 fusion.53
  67.6 3.4 fusion.116
  71.0 3.4 fusion.50
  74.4 3.5 fusion.118
  77.9 0.1 constant_dynamic-slice_fusion.2
  78.0 1.3 collective-permute-start.1
  79.3 14.9 %collective-permute-done.1 = f32[64,2560]{1,0:T(8,128)S(1)} collective-permute-done((f32[64,2560]{1,0:T(8,128)S(1)}, f32[64,2560]{1,0:T(8,128)S(1)}, u32[]{:S(2)}, u32[]{:S(2)}) %collective-permute-start.1) | collective-permute-done | bytes 655392 | tf_op jit(solution)/shard_map/ppermute | solution.py:33
  94.1 0.2 fusion.56
  94.4 0.9 fusion.58
  95.3 0.3 reduce-scatter.2.cloned.1.call-start
  95.6 0.1 eq.67
  95.7 0.7 slice_convert_fusion
  96.5 0.2 convolution_convert_fusion.3
  96.7 0.2 fusion.64
  96.9 53.5 %all-gather.11.cloned.1.call-done = bf16[1,1024,2560]{2,1,0:T(8,128)(2,1)} async-done(((bf16[1,128,2560]{2,1,0:T(8,128)(2,1)}), bf16[1,1024,2560]{2,1,0:T(8,128)(2,1)}) %all-gather.11.cloned.1.call-update) | async-done | bytes 5242896 | tf_op jit(solution)/shard_map/all_gather | solution.py:86
  150.4 6.3 %convolution_convert_fusion = bf16[8,128,2560]{2,1,0:T(8,128)(2,1)} fusion(pred[8,128,128]{2,1,0:T(32,128)(4,1)S(1)} %fusion.64, bf16[8,128,2560]{2,1,0:T(8,128)(2,1)} %bitcast.254), kind=kOutput, calls=%fused_computation.16 | convolution fusion | flops 673710080 | bytes 10616832 | tf_op jit(solution)/shard_map/sct,std->scd/dot_general | solution.py:124
  156.8 81.3 %all-gather.9.cloned.1.call-done = bf16[1024,2560]{1,0:T(8,128)(2,1)} async-done(((bf16[64,2560]{1,0:T(8,128)(2,1)}), bf16[1024,2560]{1,0:T(8,128)(2,1)}) %all-gather.9.cloned.1.call-update) | async-done | bytes 5242896 | tf_op jit(solution)/shard_map/all_gather | solution.py:168
  238.1 4.1 convolution_convert_fusion.2
  242.3 8.5 %fusion.1 = f32[2,8,64,768]{3,2,1,0:T(8,128)S(1)} fusion(bf16[2,2560,768]{2,1,0:T(8,128)(2,1)} %param.25, bf16[8,2,64,2560]{3,2,1,0:T(8,128)(2,1)S(1)} %bitcast.245), kind=kOutput, calls=%fused_computation.1 | convolution fusion | flops 4026531840 | bytes 16252928 | tf_op jit(solution)/shard_map/sjcd,jdf->sjcf/dot_general | solution.py:191
  250.8 5.9 %fusion.3 = f32[2,8,64,768]{3,2,1,0:T(8,128)} fusion(bf16[2,2560,768]{2,1,0:T(8,128)(2,1)S(1)} %bitcast.264, bf16[8,2,64,2560]{3,2,1,0:T(8,128)(2,1)S(1)} %bitcast.246), kind=kOutput, calls=%fused_computation.3 | convolution fusion | flops 4026531840 | bytes 16252928 | tf_op jit(solution)/shard_map/sjcd,jdf->sjcf/dot_general | solution.py:190
  256.7 1.5 fusion.117
  258.3 12.4 %fusion.22 = (f32[8,2,64]{2,0,1:T(8,128)S(1)}, bf16[8,2,64,768]{3,2,0,1:T(8,128)(2,1)}, f32[2,8,64,768]{3,2,1,0:T(8,128)}) fusion(f32[2,8,64,768]{3,2,1,0:T(8,128)S(1)} %fusion.1, f32[2,8,64,768]{3,2,1,0:T(8,128)} %fusion.3, bf16[2,768,2560]{2,1,0:T(8,128)(2,1)} %param.26, bf16[8,2,64,2560]{3,2,1,0:T(8,128)(2,1)} %bitcast.242), kind=kOutput, calls=%fused_computation.28 | convolution fusion | flops 4033608704 | bytes 24121344 | tf_op jit(solution)/shard_map/sjcd,jfd->sjcf/dot_general | solution.py:172
  270.7 8.0 %fusion.15 = bf16[8,2,64,2560]{3,2,0,1:T(8,128)(2,1)S(1)} fusion(bf16[8,2,64,768]{3,2,0,1:T(8,128)(2,1)} %get-tuple-element.10, bf16[2,768,2560]{2,1,0:T(8,128)(2,1)} %param.26), kind=kOutput, calls=%fused_computation.19 | convolution fusion | flops 4029153280 | bytes 14680064 | tf_op jit(solution)/shard_map/sjcf,jfd->sjcd/dot_general | solution.py:194
  278.7 0.5 copy.76
  279.2 0.2 fusion.61
  279.3 3.8 convolution_convert_fusion.1
  283.2 3.6 constant_dynamic-slice_fusion
  286.9 0.4 select_reduce_fusion
  287.3 6.4 %fusion.33 = (bf16[8,2,64,768]{3,2,0,1:T(8,128)(2,1)}, bf16[8,2,64,768]{3,2,0,1:T(8,128)(2,1)}, bf16[8,2,64,768]{3,2,0,1:T(8,128)(2,1)}) fusion(f32[2,8,64,768]{3,2,1,0:T(8,128)} %fusion.3, f32[2,8,64,768]{3,2,1,0:T(8,128)} %get-tuple-element.26, f32[8,2,64]{2,0,1:T(8,128)S(1)} %copy.81, f32[2,8,64,768]{3,2,1,0:T(8,128)S(1)} %copy-done.4, ...), kind=kLoop, calls=%fused_computation.46 | loop fusion | flops 13369344 | bytes 15732736 | tf_op jit(solution)/shard_map/convert_element_type | solution.py:210
  293.7 0.4 collective-permute-start.6
  294.1 0.1 collective-permute-start.5
  294.2 1.7 constant_dynamic-slice_fusion.1
  295.9 0.4 collective-permute-start.3
  296.3 42.6 %all-gather.2 = f32[16,2,1024]{2,1,0:T(2,128)S(1)} all-gather(f32[1,2,1024]{2,1,0:T(2,128)S(1)} %bitcast.258), channel_id=3, replica_groups=mesh['dp'=2,'ctx'=8,'exp'=2] {'ctx','exp'}, dimensions={0}, use_global_device_ids=true | all-gather | bytes 139264 | tf_op jit(solution)/shard_map/all_gather | solution.py:220
  338.9 0.1 bitcast_reduce_fusion
  339.2 3.5 fusion.69
  342.8 0.1 collective-permute-start.2
  342.8 7.7 %fusion.34 = f32[2,768,1280,1]{2,1,3,0:T(8,128)} fusion(bf16[8,2,64,768]{3,2,0,1:T(8,128)(2,1)} %get-tuple-element.21, s32[]{:T(128)S(6)} %select_n.54, bf16[8,2,64,2560]{3,2,1,0:T(8,128)(2,1)} %bitcast.243), kind=kOutput, calls=%fused_computation.47 | convolution fusion | flops 2013265920 | bytes 12058628 | tf_op jit(solution)/shard_map/sjcf,sjcd->jfd/dot_general | solution.py:233
  350.6 6.9 %fusion.36 = f32[2,1280,768,1]{2,1,3,0:T(8,128)} fusion(bf16[8,2,64,768]{3,2,0,1:T(8,128)(2,1)} %get-tuple-element.13, s32[]{:T(128)S(6)} %select_n.54, bf16[8,2,64,2560]{3,2,1,0:T(8,128)(2,1)S(1)} %bitcast.252), kind=kOutput, calls=%fused_computation.49 | convolution fusion | flops 2013265920 | bytes 12058628 | tf_op jit(solution)/shard_map/sjcd,sjcf->jdf/dot_general | solution.py:233
  357.5 2.3 fusion.38
  359.9 0.5 collective-permute-start.4
  360.3 0.7 add.119
  361.0 9.1 %fusion.5 = bf16[2,768,1280]{2,1,0:T(8,128)(2,1)} fusion(f32[2,768,1280,1]{2,1,3,0:T(8,128)} %fusion.34, bf16[8,2,64,768]{3,2,0,1:T(8,128)(2,1)} %collective-permute-done.6, bf16[8,2,64,1280]{3,2,0,1:T(8,128)(2,1)} %collective-permute-done.7), kind=kOutput, calls=%fused_computation.6 | convolution fusion | flops 2017198080 | bytes 15990784 | tf_op jit(solution)/shard_map/sjcf,sjcd->jfd/dot_general | solution.py:234
  370.2 6.9 %fusion.6 = bf16[2,1280,768]{2,1,0:T(8,128)(2,1)} fusion(f32[2,1280,768,1]{2,1,3,0:T(8,128)S(1)} %bitcast.266, bf16[8,2,64,1280]{3,2,0,1:T(8,128)(2,1)} %collective-permute-done.3, bf16[8,2,64,768]{3,2,0,1:T(8,128)(2,1)} %collective-permute-done.5), kind=kOutput, calls=%fused_computation.8 | convolution fusion | flops 2017198080 | bytes 15990784 | tf_op jit(solution)/shard_map/sjcd,sjcf->jdf/dot_general | solution.py:234
  377.1 6.3 %fusion.7 = bf16[2,1280,768]{2,1,0:T(8,128)(2,1)} fusion(f32[2,1280,768,1]{2,1,3,0:T(8,128)S(1)} %fusion.38, bf16[8,2,64,1280]{3,2,0,1:T(8,128)(2,1)} %collective-permute-done.3, bf16[8,2,64,768]{3,2,0,1:T(8,128)(2,1)S(1)} %collective-permute-done.4), kind=kOutput, calls=%fused_computation.10 | convolution fusion | flops 2017198080 | bytes 15990784 | tf_op jit(solution)/shard_map/sjcd,sjcf->jdf/dot_general | solution.py:234
  383.4 15.6 %reduce-scatter.2.cloned.1.call-done = bf16[64,2560]{1,0:T(8,128)(2,1)} async-done(((bf16[1024,2560]{1,0:T(8,128)(2,1)}), bf16[64,2560]{1,0:T(8,128)(2,1)}) %reduce-scatter.2.cloned.1.call-update) | async-done | bytes 327696 | tf_op jit(solution)/shard_map/reduce_scatter | solution.py:203
  399.0 1.1 fusion.59
  400.0 11.5 %all_gather.20 = bf16[128,2560]{1,0:T(8,128)(2,1)S(1)} all-gather(bf16[64,2560]{1,0:T(8,128)(2,1)S(1)} %fusion.59), channel_id=1, replica_groups=mesh['dp'=2,'ctx'=8,'exp'=2] {'exp'}, dimensions={0}, use_global_device_ids=true | all-gather | bytes 983040 | tf_op jit(solution)/shard_map/all_gather | solution.py:243
  411.6 0.8 copy.138
  (91 shorter events, 0.8 us)
Async XLA Ops:
  7.2 1.4 copy-start
  7.2 57.0 %copy-start.9 = (s32[1,128]{1,0:T(1,128)S(1)}, s32[1,128]{1,0:T(1,128)}, u32[]{:S(2)}) copy-start(s32[1,128]{1,0:T(1,128)} %param.23) | copy-start | bytes 1540
  7.2 57.2 %copy-start.11 = (bf16[1,128,8,576]{1,3,2,0:T(8,128)(2,1)S(1)}, bf16[1,128,8,576]{1,3,2,0:T(8,128)(2,1)}, u32[]{:S(2)}) copy-start(bf16[1,128,8,576]{1,3,2,0:T(8,128)(2,1)} %param.15) | copy-start | bytes 3538948
  7.2 56.3 %all-gather.7.cloned.1.call-start = ((), (), s32[]{:S(2)}) async-start(), calls=%async_computation.1 | async-start | bytes 1345536 | tf_op jit(solution)/shard_map/all_gather | solution.py:98
  10.1 8.8 %collective-permute-start = (f32[128,576]{0,1:T(8,128)S(1)}, f32[128,576]{0,1:T(8,128)S(1)}, u32[]{:S(2)}, u32[]{:S(2)}) collective-permute-start(f32[128,576]{0,1:T(8,128)S(1)} %fusion.66), channel_id=1, source_target_pairs={{0,1},{1,0},{2,3},{3,2},{4,5},{5,4},{6,7},{7,6},{8,9},{9,8},{10,11... | collective-permute-start | bytes 884744 | tf_op jit(solution)/shard_map/ppermute | solution.py:33
  21.8 128.6 %all-gather.11.cloned.1.call-start = ((), (), s32[]{:S(2)}) async-start(), calls=%async_computation.4 | async-start | bytes 5898240 | tf_op jit(solution)/shard_map/all_gather | solution.py:86
  22.6 215.5 %all-gather.9.cloned.1.call-start = ((), (), s32[]{:S(2)}) async-start(), calls=%async_computation.2 | async-start | bytes 5570560 | tf_op jit(solution)/shard_map/all_gather | solution.py:168
  67.6 3.4 copy-start.10
  67.6 3.4 copy-start.12
  74.4 4.9 %copy-start.8 = (bf16[2560]{0:T(1024)(128)(2,1)S(1)}, bf16[2560]{0:T(1024)(128)(2,1)}, u32[]{:S(2)}) copy-start(bf16[2560]{0:T(1024)(128)(2,1)} %param.20) | copy-start | bytes 15364
  74.4 19.7 %copy-start.6 = (bf16[1,128,2560]{2,1,0:T(8,128)(2,1)S(1)}, bf16[1,128,2560]{2,1,0:T(8,128)(2,1)}, u32[]{:S(2)}) copy-start(bf16[1,128,2560]{2,1,0:T(8,128)(2,1)} %param.14) | copy-start | bytes 1966084
  78.0 16.1 %collective-permute-start.1 = (f32[64,2560]{1,0:T(8,128)S(1)}, f32[64,2560]{1,0:T(8,128)S(1)}, u32[]{:S(2)}, u32[]{:S(2)}) collective-permute-start(f32[64,2560]{1,0:T(8,128)S(1)} %constant_dynamic-slice_fusion.2), channel_id=1, source_target_pairs={{0,1},{1,0},{2,3},{3,2},{4,5},{5,4},{6,7},{7,6},{8,9},{9,8},{10,11... | collective-permute-start | bytes 1966088 | tf_op jit(solution)/shard_map/ppermute | solution.py:33
  95.3 303.7 %reduce-scatter.2.cloned.1.call-start = ((), (), s32[]{:S(2)}) async-start(), calls=%async_computation.3 | async-start | bytes 5570560 | tf_op jit(solution)/shard_map/reduce_scatter | solution.py:203
  238.1 12.7 %slice-start.6 = ((s8[7864320]{0:T(1024)(128)(4,1)}), s8[4194304]{0:T(1024)(128)(4,1)S(1)}, s32[]{:S(2)}) async-start(s8[7864320]{0:T(1024)(128)(4,1)} %bitcast.263), calls=%async_computation.11 | async-start | bytes 8388608
  238.1 18.6 %slice-start = ((s8[5242880]{0:T(1024)(128)(4,1)}), s8[4194304]{0:T(1024)(128)(4,1)S(1)}, s32[]{:S(2)}) async-start(s8[5242880]{0:T(1024)(128)(4,1)} %bitcast.239), calls=%async_computation.5 | async-start | bytes 8388608
  242.2 8.5 %copy-start.2 = (bf16[8,128,2560]{2,1,0:T(8,128)(2,1)}, bf16[8,128,2560]{2,1,0:T(8,128)(2,1)S(1)}, u32[]{:S(2)}) copy-start(bf16[8,128,2560]{2,1,0:T(8,128)(2,1)S(1)} %convolution_convert_fusion.2) | copy-start | bytes 15728644
  242.2 8.5 %slice-start.7 = ((s8[7864320]{0:T(1024)(128)(4,1)}), s8[3670016]{0:T(1024)(128)(4,1)S(1)}, s32[]{:S(2)}) async-start(s8[7864320]{0:T(1024)(128)(4,1)} %bitcast.263), calls=%async_computation.12 | async-start | bytes 7340032
  242.3 14.4 %slice-start.1 = ((s8[5242880]{0:T(1024)(128)(4,1)}), s8[1048576]{0:T(1024)(128)(4,1)S(1)}, s32[]{:S(2)}) async-start(s8[5242880]{0:T(1024)(128)(4,1)} %bitcast.239), calls=%async_computation.6 | async-start | bytes 2097152
  250.8 7.6 %copy-start.3 = (f32[2,8,64,768]{3,2,1,0:T(8,128)}, f32[2,8,64,768]{3,2,1,0:T(8,128)S(1)}, u32[]{:S(2)}) copy-start(f32[2,8,64,768]{3,2,1,0:T(8,128)S(1)} %fusion.1) | copy-start | bytes 9437188
  250.8 5.9 %copy-start.7 = (bf16[2560,16]{0,1:T(8,128)(2,1)S(1)}, bf16[2560,16]{0,1:T(8,128)(2,1)}, u32[]{:S(2)}) copy-start(bf16[2560,16]{0,1:T(8,128)(2,1)} %param.21) | copy-start | bytes 245764
  283.2 4.1 copy-start.4
  283.2 11.0 %slice-start.2 = ((s8[5242880]{0:T(1024)(128)(4,1)}), s8[4194304]{0:T(1024)(128)(4,1)S(1)}, s32[]{:S(2)}) async-start(s8[5242880]{0:T(1024)(128)(4,1)} %bitcast.247), calls=%async_computation.7 | async-start | bytes 8388608
  286.9 74.2 %collective-permute-start.7 = (bf16[8,2,64,1280]{3,2,0,1:T(8,128)(2,1)}, bf16[8,2,64,1280]{3,2,0,1:T(8,128)(2,1)}, u32[]{:S(2)}, u32[]{:S(2)}) collective-permute-start(bf16[8,2,64,1280]{3,2,0,1:T(8,128)(2,1)} %constant_dynamic-slice_fusion), channel_id=1, source_target_pairs={{0,16},{16,0},{1,17},{17,1},{2,18},{18,2},{3,19},{19,3},{4,20},{20... | collective-permute-start | bytes 7864328 | tf_op jit(solution)/shard_map/ppermute | solution.py:33
  287.3 6.9 %slice-start.3 = ((s8[5242880]{0:T(1024)(128)(4,1)}), s8[1048576]{0:T(1024)(128)(4,1)S(1)}, s32[]{:S(2)}) async-start(s8[5242880]{0:T(1024)(128)(4,1)} %bitcast.247), calls=%async_computation.8 | async-start | bytes 2097152
  293.7 67.3 %collective-permute-start.6 = (bf16[8,2,64,768]{3,2,0,1:T(8,128)(2,1)}, bf16[8,2,64,768]{3,2,0,1:T(8,128)(2,1)}, u32[]{:S(2)}, u32[]{:S(2)}) collective-permute-start(bf16[8,2,64,768]{3,2,0,1:T(8,128)(2,1)} %get-tuple-element.21), channel_id=1, source_target_pairs={{0,16},{16,0},{1,17},{17,1},{2,18},{18,2},{3,19},{19,3},{4,20},{20... | collective-permute-start | bytes 4718600 | tf_op jit(solution)/shard_map/ppermute | solution.py:33
  294.1 76.1 %collective-permute-start.5 = (bf16[8,2,64,768]{3,2,0,1:T(8,128)(2,1)}, bf16[8,2,64,768]{3,2,0,1:T(8,128)(2,1)}, u32[]{:S(2)}, u32[]{:S(2)}) collective-permute-start(bf16[8,2,64,768]{3,2,0,1:T(8,128)(2,1)} %get-tuple-element.13), channel_id=1, source_target_pairs={{0,16},{16,0},{1,17},{17,1},{2,18},{18,2},{3,19},{19,3},{4,20},{20... | collective-permute-start | bytes 4718600 | tf_op jit(solution)/shard_map/ppermute | solution.py:33
  295.9 74.3 %collective-permute-start.3 = (bf16[8,2,64,1280]{3,2,0,1:T(8,128)(2,1)}, bf16[8,2,64,1280]{3,2,0,1:T(8,128)(2,1)}, u32[]{:S(2)}, u32[]{:S(2)}) collective-permute-start(bf16[8,2,64,1280]{3,2,0,1:T(8,128)(2,1)} %constant_dynamic-slice_fusion.1), channel_id=1, source_target_pairs={{0,16},{16,0},{1,17},{17,1},{2,18},{18,2},{3,19},{19,3},{4,20},{20... | collective-permute-start | bytes 7864328 | tf_op jit(solution)/shard_map/ppermute | solution.py:33
  342.7 7.8 %slice-start.4 = ((s8[5242880]{0:T(1024)(128)(4,1)}), s8[1048576]{0:T(1024)(128)(4,1)S(1)}, s32[]{:S(2)}) async-start(s8[5242880]{0:T(1024)(128)(4,1)} %bitcast.250), calls=%async_computation.9 | async-start | bytes 2097152
  342.7 7.8 %slice-start.5 = ((s8[5242880]{0:T(1024)(128)(4,1)}), s8[4194304]{0:T(1024)(128)(4,1)S(1)}, s32[]{:S(2)}) async-start(s8[5242880]{0:T(1024)(128)(4,1)} %bitcast.250), calls=%async_computation.10 | async-start | bytes 8388608
  342.8 17.1 %collective-permute-start.2 = (f32[2560,16]{0,1:T(8,128)S(1)}, f32[2560,16]{0,1:T(8,128)S(1)}, u32[]{:S(2)}, u32[]{:S(2)}) collective-permute-start(f32[2560,16]{0,1:T(8,128)S(1)} %reduce_sum.118), channel_id=1, source_target_pairs={{0,16},{16,0},{1,17},{17,1},{2,18},{18,2},{3,19},{19,3},{4,20},{20... | collective-permute-start | bytes 491528 | tf_op jit(solution)/shard_map/ppermute | solution.py:33
  350.5 7.0 %copy-start.5 = (bf16[8,2,64,768]{3,2,0,1:T(8,128)(2,1)S(1)}, bf16[8,2,64,768]{3,2,0,1:T(8,128)(2,1)}, u32[]{:S(2)}) copy-start(bf16[8,2,64,768]{3,2,0,1:T(8,128)(2,1)} %get-tuple-element.14) | copy-start | bytes 4718596
  359.9 17.2 %collective-permute-start.4 = (bf16[8,2,64,768]{3,2,0,1:T(8,128)(2,1)S(1)}, bf16[8,2,64,768]{3,2,0,1:T(8,128)(2,1)S(1)}, u32[]{:S(2)}, u32[]{:S(2)}) collective-permute-start(bf16[8,2,64,768]{3,2,0,1:T(8,128)(2,1)S(1)} %copy-done.5), channel_id=1, source_target_pairs={{0,16},{16,0},{1,17},{17,1},{2,18},{18,2},{3,19},{19,3},{4,20},{20... | collective-permute-start | bytes 4718600 | tf_op jit(solution)/shard_map/ppermute | solution.py:33
  360.3 9.8 %slice-start.8 = ((s8[7864320]{0:T(1024)(128)(4,1)}), s8[4194304]{0:T(1024)(128)(4,1)S(1)}, s32[]{:S(2)}) async-start(s8[7864320]{0:T(1024)(128)(4,1)} %bitcast.265), calls=%async_computation.13 | async-start | bytes 8388608
  361.0 9.2 %slice-start.9 = ((s8[7864320]{0:T(1024)(128)(4,1)}), s8[3670016]{0:T(1024)(128)(4,1)S(1)}, s32[]{:S(2)}) async-start(s8[7864320]{0:T(1024)(128)(4,1)} %bitcast.265), calls=%async_computation.14 | async-start | bytes 7340032
  377.1 35.3 %copy-start.1 = (bf16[1280,576]{0,1:T(8,128)(2,1)S(1)}, bf16[1280,576]{0,1:T(8,128)(2,1)}, u32[]{:S(2)}) copy-start(bf16[1280,576]{0,1:T(8,128)(2,1)} %param.16) | copy-start | bytes 4423684
Sparse Core Ops, SparseCore 0:
  21.9 41.5 all-gather.6
  65.7 84.7 all-gather.10
  153.8 84.2 all-gather.8
  283.3 115.6 reduce-scatter.1
